TPU v7x, 32 devices: a whole 2x2x4 slice. The times are simulated.
32 devices in a mesh: grp: 4 (over y, core), in: 8 (over z, x).
Axes of the slice: x: 2, y: 2, z: 4, core: 2. Of those that a mesh axis runs over, the one named last changes fastest.
Arguments:
- tokens: bfloat16 [32, 144, 8192], P(('grp', 'in')), may hold values from -6 to 6
- queries: bfloat16 [32, 144, 1024], P(('grp', 'in')), may hold values from -120 to 120
- key_rows: bfloat16 [32, 144, 128], P(('grp', 'in')), may hold values from -5 to 5
- cotangent: bfloat16 [32, 144, 1024], P(('grp', 'in')), may hold values from -6 to 6
- segments: int32 [32, 144], P(('grp', 'in')), may hold values from 0 to 3, as said below
- levels: bfloat16 [64, 128, 128], P('in'), may hold values from -127 to 127, as said below
- scales: bfloat16 [64, 128], P('in'), may hold values from 4.9829483e-05 to 0.00049972534
Outputs:
- attended: bfloat16 [32, 144, 1024], P(('grp', 'in'))
- query_grad: bfloat16 [32, 144, 1024], P(('grp', 'in'))
- key_grad: bfloat16 [32, 144, 128], P(('grp', 'in'))
- value_weight_grad: float32 [128, 8192], P('grp', 'in')
Inputs may be any that keep to these rules, and one draw needn't show every extreme that they name: `segments`: within each sequence the numbers never fall, start at 0, grow by one at each of 3 distinct positions, and the last two positions share a document. `levels`: whole numbers.
All inputs are finite; a program needn't handle non-finite values.
Results may differ from a plain program's by a relative error of at most 0.0085.
Values may be sent and summed in bfloat16 or wider, within the bound.
A program may use at most 64 MiB of HBM per device.

v0:
```python
import jax
import jax.numpy as jnp
from jax import lax
from jax.sharding import PartitionSpec as P


def per_device(tokens, queries, key_rows, cotangent, segments, levels, scales):
    tokens_one = tokens[0]
    length = tokens_one.shape[0]
    head_size = key_rows.shape[2]
    heads = queries.shape[2] // head_size
    factor = head_size ** (-0.5)
    query_heads = queries[0].reshape(length, heads, head_size)
    cot_heads = cotangent[0].reshape(length, heads, head_size)
    keys_one = key_rows[0]
    segment_row = segments[0]
    scores = (
        jnp.einsum("sgd,td->gst", query_heads, keys_one, preferred_element_type=jnp.float32)
        * factor
    )
    position = jnp.arange(length)
    allowed = (position[:, None] >= position[None, :]) & (
        segment_row[:, None] == segment_row[None, :]
    )
    scores = jnp.where(allowed[None], scores, -jnp.inf)
    row_top = jnp.max(scores, axis=-1, keepdims=True)
    expo = jnp.exp(scores - row_top)
    probs = expo / jnp.sum(expo, axis=-1, keepdims=True)
    probs_low = probs.astype(jnp.bfloat16)
    level_piece = lax.all_gather(levels, "in", axis=0, tiled=True)
    scale_piece = lax.all_gather(scales, "in", axis=0, tiled=True)
    block_count = level_piece.shape[0]
    block_rows = level_piece.shape[1]
    dequant = level_piece.astype(jnp.float32) * scale_piece.astype(jnp.float32)[:, None, :]
    dequant = dequant.reshape(block_count * block_rows, head_size).astype(jnp.bfloat16)
    values = jnp.dot(tokens_one, dequant, preferred_element_type=jnp.float32).astype(jnp.bfloat16)
    attended = jnp.einsum("gst,td->sgd", probs_low, values, preferred_element_type=jnp.float32)
    attended = attended.reshape(length, heads * head_size).astype(jnp.bfloat16)
    value_grad = jnp.einsum(
        "gst,sgd->td", probs_low, cot_heads, preferred_element_type=jnp.float32
    ).astype(jnp.bfloat16)
    term = jnp.dot(value_grad.T, tokens_one, preferred_element_type=jnp.float32).astype(
        jnp.bfloat16
    )
    received = lax.all_to_all(term[None], "in", split_axis=2, concat_axis=0, tiled=True)
    group_total = jnp.sum(received.astype(jnp.float32), axis=0)
    group_low = group_total.astype(jnp.bfloat16)
    prob_grad = jnp.einsum("sgd,td->gst", cot_heads, values, preferred_element_type=jnp.float32)
    centre = jnp.sum(probs * prob_grad, axis=-1, keepdims=True)
    score_grad = (probs * (prob_grad - centre) * factor).astype(jnp.bfloat16)
    query_grad = jnp.einsum("gst,td->sgd", score_grad, keys_one, preferred_element_type=jnp.float32)
    query_grad = query_grad.reshape(length, heads * head_size).astype(jnp.bfloat16)
    key_grad = jnp.einsum(
        "gst,sgd->td", score_grad, query_heads, preferred_element_type=jnp.float32
    ).astype(jnp.bfloat16)
    gathered = lax.all_to_all(group_low[None], "grp", split_axis=1, concat_axis=0, tiled=True)
    cross_total = jnp.sum(gathered.astype(jnp.float32), axis=0)
    replicas = lax.axis_size("grp") * lax.axis_size("in")
    weight_grad = cross_total / replicas
    return (attended[None], query_grad[None], key_grad[None], weight_grad)


def solution(mesh):
    placed = (
        P(("grp", "in"), None, None),
        P(("grp", "in"), None, None),
        P(("grp", "in"), None, None),
        P(("grp", "in"), None, None),
        P(("grp", "in"), None),
        P("in", None, None),
        P("in", None),
    )
    return jax.shard_map(
        per_device,
        mesh=mesh,
        in_specs=placed,
        out_specs=(
            P(("grp", "in"), None, None),
            P(("grp", "in"), None, None),
            P(("grp", "in"), None, None),
            P("grp", "in"),
        ),
        check_vma=False,
    )
```

profile of v0, /device:TPU:0, one launch (start us, length us, event | category | flops | bytes accessed | tf_op | source)
XLA Modules:
  0.0 196.7 jit_solution(16521582049681296433)
XLA Ops:
  7.2 0.0 copy-start
  7.2 0.0 copy-start.2
  7.2 0.0 copy-start.4
  7.2 0.0 all-gather.2.cloned.1.call-start
  7.2 0.7 all-gather.2.cloned.1.call-update
  7.9 1.0 copy.59
  8.9 1.0 copy.60
  10.0 0.0 copy-done.2
  10.0 0.1 fusion.40
  10.1 0.0 copy-done.4
  10.1 1.5 fusion.66
  11.6 0.0 copy-done
  11.6 3.7 %fusion.2 = bf16[1,128,8192]{2,1,0:T(8,128)(2,1)} fusion(bf16[1,144,8192]{2,1,0:T(8,128)(2,1)S(1)} %copy-done, bf16[144,8,128]{2,1,0:T(8,128)(2,1)S(1)} %bitcast.86, f32[8,144,144]{1,2,0:T(8,128)} %get-tuple-element.5, f32[8,144]{1,0:T(8,128)S(1)} %get-tuple-element.4), kind=kOutput, calls=%fused_computation.3 | convolution fusion | flops 345856000 | bytes 5419520 | tf_op jit(solution)/shard_map/dot_general | solution.py:42
  15.4 9.5 %copy.50 = bf16[1,128,8192]{1,0,2:T(2,128)(2,1)} copy(bf16[1,128,8192]{2,1,0:T(8,128)(2,1)} %fusion.2) | data formatting | bytes 4194304 | tf_op jit(solution)/shard_map/broadcast_in_dim | solution.py:45
  24.9 0.5 broadcast.57
  25.4 46.6 %reduce.4 = bf16[8192,128]{1,0:T(8,128)(2,1)} reduce(bf16[8192,1,128]{2,1,0:T(2,128)(2,1)} %bitcast.82, bf16[]{:T(256)} %broadcast.57), dimensions={1}, to_apply=%bitcast.71.reduce_sub_computation | reduce | bytes 4194306
  72.0 5.8 %reshape.92 = bf16[8,2,65536]{2,1,0:T(2,128)(2,1)} reshape(bf16[8192,128]{1,0:T(8,128)(2,1)} %reduce.4) | data formatting | bytes 4194304
  77.8 0.0 copy-start.3
  77.8 7.4 %all-to-all-start = ((bf16[8,2,65536]{2,1,0:T(2,128)(2,1)}), bf16[8,2,65536]{2,1,0:T(2,128)(2,1)}, u32[]{:S(2)}, u32[]{:S(2)}) async-start(bf16[8,2,65536]{2,1,0:T(2,128)(2,1)} %reshape.92), calls=%async_computation | async-start | bytes 4194304 | tf_op jit(solution)/shard_map/all_to_all | solution.py:45
  85.1 0.0 copy-done.3
  85.1 66.7 %all_gather.7 = bf16[64,128]{1,0:T(8,128)(2,1)S(1)} all-gather(bf16[8,128]{1,0:T(8,128)(2,1)S(1)} %copy-done.3), channel_id=1, replica_groups=mesh['grp'=4,'in'=8] {'in'}, dimensions={0}, use_global_device_ids=true | all-gather | bytes 18432 | tf_op jit(solution)/shard_map/all_gather | solution.py:31
  151.9 0.0 all-gather.2.cloned.1.call-done
  151.9 2.2 %multiply_convert_fusion = bf16[64,128,128]{2,1,0:T(8,128)(2,1)S(1)} fusion(bf16[64,128,128]{2,1,0:T(8,128)(2,1)} %all-gather.2.cloned.1.call-done, f32[64,128]{1,0:T(8,128)S(1)} %convert_element_type.75), kind=kLoop, calls=%fused_computation.4 | loop fusion | flops 3145728 | bytes 4227072 | tf_op jit(solution)/shard_map/convert_element_type | solution.py:35
  154.1 0.8 fusion.22
  154.9 1.5 fusion.14
  156.4 1.4 convolution_bitcast_fusion
  157.7 0.0 all-to-all-done
  157.7 6.8 %reshape.93 = bf16[8192,1,128]{2,1,0:T(2,128)(2,1)} reshape(bf16[8,2,65536]{2,1,0:T(2,128)(2,1)} %all-to-all-done) | data formatting | bytes 4194304
  164.6 3.8 %copy.57 = bf16[1,128,8192]{1,2,0:T(8,128)(2,1)} copy(bf16[1,128,8192]{1,0,2:T(2,128)(2,1)} %bitcast.83) | data formatting | bytes 4194304
  168.3 2.0 %reduce_sum.41 = bf16[128,1024]{0,1:T(8,128)(2,1)S(1)} reduce(bf16[128,8,1024]{0,2,1:T(8,128)(2,1)} %bitcast.84, bf16[]{:T(256)} %constant.9.clone.1), dimensions={1}, to_apply=%region_3.4 | reduce | flops 917504 | bytes 2359298 | tf_op jit(solution)/shard_map/reduce_sum | solution.py:46
  170.3 0.5 copy.52
  170.8 2.2 %reduce.5 = bf16[128,1024]{1,0:T(8,128)(2,1)S(1)} reduce(bf16[128,1,1024]{2,1,0:T(2,128)(2,1)S(1)} %bitcast.88, bf16[]{:T(256)} %broadcast.57), dimensions={1}, to_apply=%bitcast.73.reduce_sub_computation | reduce | bytes 524290
  173.0 0.9 reshape.94
  173.8 4.0 %all-to-all-start.1 = ((bf16[4,2,16384]{2,1,0:T(2,128)(2,1)}), bf16[4,2,16384]{2,1,0:T(2,128)(2,1)}, u32[]{:S(2)}, u32[]{:S(2)}) async-start(bf16[4,2,16384]{2,1,0:T(2,128)(2,1)} %reshape.94), calls=%async_computation.1 | async-start | bytes 524288 | tf_op jit(solution)/shard_map/all_to_all | solution.py:56
  177.9 0.0 copy-start.1
  177.9 3.7 %fusion.15 = bf16[144,8,128]{2,0,1:T(8,128)(2,1)} fusion(f32[8,144,144]{1,2,0:T(8,128)} %convolution_bitcast_fusion, bf16[1,144,128]{2,1,0:T(8,128)(2,1)S(1)} %copy-done.4, f32[8,144,144]{1,2,0:T(8,128)} %get-tuple-element.5, f32[8,144]{1,0:T(8,128)S(1)} %get-tuple-element.4), kind=kOutput, calls=%fused_computation.21 | convolution fusion | flops 43777296 | bytes 1663488 | tf_op jit(solution)/shard_map/gst,td->sgd/dot_general | solution.py:51
  181.6 0.0 copy-done.1
  181.6 0.1 copy.44
  181.6 0.8 convert_element_type.82
  182.5 1.0 copy.47
  183.5 0.8 convert_element_type.86
  184.4 3.5 %fusion.21 = bf16[1,144,128]{2,1,0:T(8,128)(2,1)} fusion(f32[8,144,144]{1,2,0:T(8,128)} %convolution_bitcast_fusion, bf16[144,8,128]{2,1,0:T(8,128)(2,1)S(1)} %bitcast.96, f32[8,144,144]{1,2,0:T(8,128)} %get-tuple-element.5, f32[8,144]{1,0:T(8,128)S(1)} %get-tuple-element.4), kind=kOutput, calls=%fused_computation.27 | convolution fusion | flops 43648272 | bytes 1663488 | tf_op jit(solution)/shard_map/gst,sgd->td/dot_general | solution.py:53
  187.9 0.0 all-to-all-done.1
  187.9 1.2 reshape.95
  189.1 0.1 copy.58
  189.2 0.7 broadcast_multiply_fusion
  (2 shorter events, 0.0 us)
Async XLA Ops:
  7.2 4.5 %copy-start = (bf16[1,144,8192]{2,1,0:T(8,128)(2,1)S(1)}, bf16[1,144,8192]{2,1,0:T(8,128)(2,1)}, u32[]{:S(2)}) copy-start(bf16[1,144,8192]{2,1,0:T(8,128)(2,1)} %param.7) | copy-start | bytes 7077892
  7.2 2.8 %copy-start.2 = (s32[1,144]{1,0:T(1,128)S(1)}, s32[1,144]{1,0:T(1,128)}, u32[]{:S(2)}) copy-start(s32[1,144]{1,0:T(1,128)} %param.11) | copy-start | bytes 1732
  7.2 2.9 %copy-start.4 = (bf16[1,144,128]{2,1,0:T(8,128)(2,1)S(1)}, bf16[1,144,128]{2,1,0:T(8,128)(2,1)}, u32[]{:S(2)}) copy-start(bf16[1,144,128]{2,1,0:T(8,128)(2,1)} %param.9) | copy-start | bytes 110596
  7.2 144.7 %all-gather.2.cloned.1.call-start = ((), (), s32[]{:S(2)}) async-start(), calls=%async_computation.2 | async-start | bytes 2359296 | tf_op jit(solution)/shard_map/all_gather | solution.py:30
  77.8 7.4 %copy-start.3 = (bf16[8,128]{1,0:T(8,128)(2,1)S(1)}, bf16[8,128]{1,0:T(8,128)(2,1)}, u32[]{:S(2)}) copy-start(bf16[8,128]{1,0:T(8,128)(2,1)} %param.13) | copy-start | bytes 6148
  77.8 80.0 %all-to-all-start = ((bf16[8,2,65536]{2,1,0:T(2,128)(2,1)}), bf16[8,2,65536]{2,1,0:T(2,128)(2,1)}, u32[]{:S(2)}, u32[]{:S(2)}) async-start(bf16[8,2,65536]{2,1,0:T(2,128)(2,1)} %reshape.92), calls=%async_computation | async-start | bytes 4194304 | tf_op jit(solution)/shard_map/all_to_all | solution.py:45
  173.8 14.0 %all-to-all-start.1 = ((bf16[4,2,16384]{2,1,0:T(2,128)(2,1)}), bf16[4,2,16384]{2,1,0:T(2,128)(2,1)}, u32[]{:S(2)}, u32[]{:S(2)}) async-start(bf16[4,2,16384]{2,1,0:T(2,128)(2,1)} %reshape.94), calls=%async_computation.1 | async-start | bytes 524288 | tf_op jit(solution)/shard_map/all_to_all | solution.py:56
  177.9 3.7 %copy-start.1 = (bf16[144,8,128]{2,0,1:T(8,128)(2,1)S(1)}, bf16[144,8,128]{2,0,1:T(8,128)(2,1)}, u32[]{:S(2)}) copy-start(bf16[144,8,128]{2,0,1:T(8,128)(2,1)} %fusion.14) | copy-start | bytes 884740
Sparse Core Ops, SparseCore 0:
  10.2 51.9 all-gather.1
where the time goes:
time: 198 us; the launch traced here: 197 us
  blocking collectives  66.7 us (34%)
  other arithmetic  53.7 us (27%)
  local copies, waits for them, and re-layouts  33.9 us (17%)
  matrix products  16.1 us (8%)
  between operations  14.2 us (7%)
  starting transfers between devices  11.4 us (6%)
    all_gather x1, blocking collectives, per_device(): scale_piece = lax.all_gather(scales, 'in', axis=0, tiled=True)  66.7 us
    unnamed x2, other arithmetic  48.7 us
    unnamed x19, local copies, waits for them, and re-layouts  21.1 us
    broadcast_in_dim x1, local copies, waits for them, and re-layouts, per_device(): term[None]  9.51 us
    all_to_all x1, starting transfers between devices, per_device(): lax.all_to_all(term[None], 'in', split_axis=2, concat_axis=0, tiled=True)  7.36 us
    all_to_all x1, starting transfers between devices, per_device(): lax.all_to_all(group_low[None], 'grp', split_axis=1, concat_axis=0, tiled...  4.04 us
  transfers between devices with their start and end apart: 3, of which 0 were waited for; matrix products, arithmetic and copies ran while one was open for 44% of the time, Pallas kernels for 0%

commit v1 on v0

v1 whole, which is shorter than its diff:
```python
import functools
import math

import jax
import jax.numpy as jnp
from jax import lax
from jax.experimental import pallas as pl
from jax.experimental.pallas import tpu as pltpu
from jax.sharding import PartitionSpec as P

MESH = pl.DeviceIdType.MESH
F32 = jnp.float32
BF16 = jnp.bfloat16


def dot(a, b, ca, cb):
    return lax.dot_general(a, b, (((ca,), (cb,)), ((), ())), preferred_element_type=F32)


def remote(src, dst, send, recv, dev):
    return pltpu.make_async_remote_copy(
        src_ref=src, dst_ref=dst, send_sem=send, recv_sem=recv, device_id=dev, device_id_type=MESH
    )


def kernel(
    dims,
    tok_hbm, q_hbm, k_ref, cot_hbm, seg_ref, lev_hbm, sca_ref,
    att_hbm, qg_hbm, kg_hbm, wg_hbm,
    tok, qs, cs, lev, wbuf, probs, probs_low, sg_low,
    term_send, term_own, term_recv, sum_core, y_recv, sum_y, x_recv, sum_x, z_recv,
    att_v, qg_v, kg_v, wg_v,
    in_sem, q_sem, c_sem, out_sem,
    core_s, core_r, ys_s, ys_r, xs_s, xs_r, zs_s, zs_r,
    gz_s, gz_r, gx_s, gx_r, gc_s, gc_r,
):
    Y, X, Z, heads, L, hd = dims
    r, c_w = wg_v.shape
    g, i = lax.axis_index("grp"), lax.axis_index("in")
    y, c = g // 2, lax.rem(g, 2)
    z, x = i // X, lax.rem(i, X)
    other = 1 - c
    core_dev = (y * 2 + other, i)

    def y_dev(d):
        return (lax.rem(y + d, Y) * 2 + c, i)

    def x_dev(d):
        return (g, z * X + lax.rem(x + d, X))

    def z_dev(d):
        return (g, lax.rem(z + d, Z) * X + x)

    lev_cp = pltpu.make_async_copy(lev_hbm, lev, in_sem.at[0])
    lev_cp.start()
    q_cps, c_cps = [], []
    for h in range(heads):
        q_cps.append(pltpu.make_async_copy(
            q_hbm.at[0, :, pl.ds(h * hd, hd)], qs.at[pl.ds(h * L, L)], q_sem.at[h]))
        q_cps[-1].start()
    for h in range(heads):
        c_cps.append(pltpu.make_async_copy(
            cot_hbm.at[0, :, pl.ds(h * hd, hd)], cs.at[pl.ds(h * L, L)], c_sem.at[h]))
        c_cps[-1].start()
    tok_cp = pltpu.make_async_copy(tok_hbm.at[0], tok, in_sem.at[1])
    tok_cp.start()

    barrier = pltpu.get_barrier_semaphore()
    peers = [core_dev]
    peers += [y_dev(d) for d in range(1, Y)]
    peers += [x_dev(d) for d in range(1, X)]
    peers += [z_dev(d) for d in range(1, Z)]
    for dev in peers:
        pl.semaphore_signal(barrier, inc=1, device_id=dev, device_id_type=MESH)

    lev_cp.wait()
    blocks, block_rows = lev.shape[0], lev.shape[1]
    sca = sca_ref[...].astype(F32)
    if blocks > 1:
        hb = blocks // 2
        s_half = jnp.where(c == 0, sca[:hb], sca[hb:])
        own_w = lev[pl.ds(c * hb, hb)].astype(F32) * s_half[:, None, :]
        own_w = own_w.reshape(hb * block_rows, hd)
    else:
        hr = block_rows // 2
        own_w = lev[0, pl.ds(pl.multiple_of(c * hr, hr), hr)].astype(F32) * sca
    wbuf[i, c] = own_w.astype(BF16)

    pl.semaphore_wait(barrier, len(peers))

    sends = []

    def start(cp):
        cp.start()
        sends.append(cp)

    def piece(d, e):
        return lax.rem(z + Z - d, Z) * X + lax.rem(x + X - e, X)

    def forward_core(d, e):
        p = piece(d, e)
        start(remote(wbuf.at[p, c], wbuf.at[p, c], gc_s.at[d, e], gc_r.at[d, e], core_dev))

    def forward_x(d):
        p = piece(d, 0)
        for e in range(1, X):
            start(remote(wbuf.at[p, c], wbuf.at[p, c], gx_s.at[d, e], gx_r.at[d, e], x_dev(e)))

    def wait_z(d):
        p = piece(d, 0)
        remote(wbuf.at[p, c], wbuf.at[p, c], gz_s.at[d], gz_r.at[d], z_dev(d)).wait_recv()

    def wait_x(d, e):
        p = piece(d, e)
        remote(wbuf.at[p, c], wbuf.at[p, c], gx_s.at[d, e], gx_r.at[d, e], x_dev(e)).wait_recv()

    def wait_core(d, e):
        p = piece(d, e)
        remote(wbuf.at[p, other], wbuf.at[p, other], gc_s.at[d, e], gc_r.at[d, e], core_dev).wait_recv()

    for d in range(1, Z):
        start(remote(wbuf.at[i, c], wbuf.at[i, c], gz_s.at[d], gz_r.at[d], z_dev(d)))
    forward_x(0)
    forward_core(0, 0)

    wide = heads * L
    factor = hd ** -0.5
    keys = k_ref[0]
    lane = lax.broadcasted_iota(jnp.int32, (1, wide), 1)
    s_pos = lane
    for h in range(1, heads):
        s_pos = jnp.where(lane >= h * L, lane - h * L, s_pos)
    t_pos = lax.broadcasted_iota(jnp.int32, (L, 1), 0)
    seg_row = seg_ref[...].astype(F32)
    sq_r = lax.broadcasted_iota(jnp.int32, (L, L), 0)
    sq_c = lax.broadcasted_iota(jnp.int32, (L, L), 1)
    seg_col = jnp.sum(jnp.where(sq_r == sq_c, seg_row, 0.0), axis=1, keepdims=True)
    seg_wide = jnp.sum(jnp.where(t_pos == s_pos, seg_col, 0.0), axis=0, keepdims=True)
    allowed = (t_pos <= s_pos) & (seg_col == seg_wide)
    for cp in q_cps:
        cp.wait()
    scores = jnp.where(allowed, dot(keys, qs[...], 1, 1) * factor, -jnp.inf)
    expo = jnp.exp(scores - jnp.max(scores, axis=0, keepdims=True))
    pr = expo * (1.0 / jnp.sum(expo, axis=0, keepdims=True))
    probs[...] = pr
    probs_low[...] = pr.astype(BF16)
    for cp in c_cps:
        cp.wait()
    vg = dot(probs_low[...], cs[...], 1, 0).astype(BF16).astype(F32)
    vg_t = vg.T.reshape(Y, 2, r, L)
    mine = jnp.where(c == 0, vg_t[:, 0], vg_t[:, 1]).reshape(Y * r, L)
    theirs = jnp.where(c == 0, vg_t[:, 1], vg_t[:, 0]).reshape(Y * r, L)
    vg_rows = jnp.concatenate([theirs, mine], axis=0).astype(BF16)

    tok_cp.wait()
    half = Y * r
    for zz in range(Z):
        for xx in range(X):
            at = (zz * X + xx) * c_w
            t = dot(vg_rows, tok[:, at:at + c_w], 1, 0)
            term_send[zz, :, xx] = t[:half].reshape(Y, r, c_w).astype(BF16)
            term_own[zz, :, xx] = t[half:].reshape(Y, r, c_w)
        start(remote(term_send.at[zz], term_recv.at[zz], core_s.at[zz], core_r.at[zz], core_dev))

    for zz in range(Z):
        remote(term_send.at[zz], term_recv.at[zz], core_s.at[zz], core_r.at[zz], core_dev).wait_recv()
        sum_core[zz] = (term_own[zz] + term_recv[zz].astype(F32)).astype(BF16)
        for d in range(1, Y):
            start(remote(sum_core.at[zz, lax.rem(y + d, Y)], y_recv.at[zz, d],
                         ys_s.at[zz, d], ys_r.at[zz, d], y_dev(d)))

    for zz in range(Z):
        total = sum_core[zz, y].astype(F32)
        for d in range(1, Y):
            remote(y_recv.at[zz, d], y_recv.at[zz, d], ys_s.at[zz, d], ys_r.at[zz, d], y_dev(d)).wait_recv()
            total = total + y_recv[zz, d].astype(F32)
        sum_y[zz] = total.astype(BF16)
        for d in range(1, X):
            start(remote(sum_y.at[zz, lax.rem(x + d, X)], x_recv.at[zz, d],
                         xs_s.at[zz, d], xs_r.at[zz, d], x_dev(d)))
        if zz + 1 < Z:
            wait_z(zz + 1)
            forward_x(zz + 1)
            forward_core(zz + 1, 0)

    for zz in range(Z):
        total = sum_y[zz, x].astype(F32)
        for d in range(1, X):
            remote(x_recv.at[zz, d], x_recv.at[zz, d], xs_s.at[zz, d], xs_r.at[zz, d], x_dev(d)).wait_recv()
            total = total + x_recv[zz, d].astype(F32)
        sum_x[zz] = total.astype(BF16)
    for d in range(1, Z):
        start(remote(sum_x.at[lax.rem(z + d, Z)], z_recv.at[d], zs_s.at[d], zs_r.at[d], z_dev(d)))

    values = jnp.zeros((L, hd), F32)
    piece_rows = 2 * wbuf.shape[2]
    for d in range(Z):
        for e in range(1, X):
            wait_x(d, e)
            forward_core(d, e)
        if d:
            for e in range(X):
                wait_core(d - 1, e)
                p = piece(d - 1, e)
                cols = pl.ds(pl.multiple_of(p * piece_rows, 128), piece_rows)
                values = values + dot(tok[:, cols], wbuf[p].reshape(piece_rows, hd), 1, 0)
    for e in range(X):
        wait_core(Z - 1, e)
        p = piece(Z - 1, e)
        cols = pl.ds(pl.multiple_of(p * piece_rows, 128), piece_rows)
        values = values + dot(tok[:, cols], wbuf[p].reshape(piece_rows, hd), 1, 0)
    v_low = values.astype(BF16)

    outs = []
    att = dot(probs_low[...], v_low, 0, 0).astype(BF16)
    for h in range(heads):
        att_v[:, h * hd:(h + 1) * hd] = att[h * L:(h + 1) * L]
    outs.append(pltpu.make_async_copy(att_v, att_hbm.at[0], out_sem.at[0]))
    outs[-1].start()
    pg = dot(v_low, cs[...], 1, 1)
    weighted = probs[...] * pg
    centre = jnp.sum(weighted, axis=0, keepdims=True)
    sg_low[...] = ((weighted - probs[...] * centre) * factor).astype(BF16)
    qg = dot(sg_low[...], keys, 0, 0).astype(BF16)
    for h in range(heads):
        qg_v[:, h * hd:(h + 1) * hd] = qg[h * L:(h + 1) * L]
    outs.append(pltpu.make_async_copy(qg_v, qg_hbm.at[0], out_sem.at[1]))
    outs[-1].start()
    kg_v[...] = dot(sg_low[...], qs[...], 1, 0).astype(BF16)
    outs.append(pltpu.make_async_copy(kg_v, kg_hbm.at[0], out_sem.at[2]))
    outs[-1].start()

    total = sum_x[z].astype(F32)
    for d in range(1, Z):
        remote(z_recv.at[d], z_recv.at[d], zs_s.at[d], zs_r.at[d], z_dev(d)).wait_recv()
        total = total + z_recv[d].astype(F32)
    wg_v[...] = total * (1.0 / (2 * Y * X * Z))
    outs.append(pltpu.make_async_copy(wg_v, wg_hbm, out_sem.at[3]))
    outs[-1].start()
    for cp in sends:
        cp.wait_send()
    for cp in outs:
        cp.wait()


def solution(mesh):
    n_grp, n_in = mesh.shape["grp"], mesh.shape["in"]
    Y = n_grp // 2
    X = 2 ** (int(math.log2(n_in)) // 3)
    Z = n_in // X

    def step(tokens, queries, key_rows, cotangent, segments, levels, scales):
        _, L, D = tokens.shape
        hd = key_rows.shape[2]
        heads = queries.shape[2] // hd
        wide = heads * L
        r, c_w = hd // n_grp, D // n_in
        half_rows = c_w // 2
        any_spec = pl.BlockSpec(memory_space=pl.ANY)
        vmem = pl.BlockSpec(memory_space=pltpu.VMEM)
        DMA = pltpu.SemaphoreType.DMA
        return pl.pallas_call(
            functools.partial(kernel, (Y, X, Z, heads, L, hd)),
            out_shape=(
                jax.ShapeDtypeStruct(queries.shape, BF16),
                jax.ShapeDtypeStruct(queries.shape, BF16),
                jax.ShapeDtypeStruct(key_rows.shape, BF16),
                jax.ShapeDtypeStruct((r, c_w), F32),
            ),
            in_specs=[any_spec, any_spec, vmem, any_spec, vmem, any_spec, vmem],
            out_specs=(any_spec,) * 4,
            scratch_shapes=[
                pltpu.VMEM((L, D), BF16),
                pltpu.VMEM((wide, hd), BF16),
                pltpu.VMEM((wide, hd), BF16),
                pltpu.VMEM(levels.shape, BF16),
                pltpu.VMEM((n_in, 2, half_rows, hd), BF16),
                pltpu.VMEM((L, wide), F32),
                pltpu.VMEM((L, wide), BF16),
                pltpu.VMEM((L, wide), BF16),
                pltpu.VMEM((Z, Y, X, r, c_w), BF16),
                pltpu.VMEM((Z, Y, X, r, c_w), F32),
                pltpu.VMEM((Z, Y, X, r, c_w), BF16),
                pltpu.VMEM((Z, Y, X, r, c_w), BF16),
                pltpu.VMEM((Z, Y, X, r, c_w), BF16),
                pltpu.VMEM((Z, X, r, c_w), BF16),
                pltpu.VMEM((Z, X, r, c_w), BF16),
                pltpu.VMEM((Z, r, c_w), BF16),
                pltpu.VMEM((Z, r, c_w), BF16),
                pltpu.VMEM((L, heads * hd), BF16),
                pltpu.VMEM((L, heads * hd), BF16),
                pltpu.VMEM((L, hd), BF16),
                pltpu.VMEM((r, c_w), F32),
                DMA((2,)), DMA((heads,)), DMA((heads,)), DMA((4,)),
                DMA((Z,)), DMA((Z,)),
                DMA((Z, Y)), DMA((Z, Y)),
                DMA((Z, X)), DMA((Z, X)),
                DMA((Z,)), DMA((Z,)),
                DMA((Z,)), DMA((Z,)),
                DMA((Z, X)), DMA((Z, X)),
                DMA((Z, X)), DMA((Z, X)),
            ],
            compiler_params=pltpu.CompilerParams(
                collective_id=0, has_side_effects=True, vmem_limit_bytes=40 * 1024 * 1024
            ),
            cost_estimate=pl.CostEstimate(
                flops=2 * L * D * hd * 2 + 12 * heads * L * L * hd,
                bytes_accessed=8_000_000, transcendentals=heads * L * L,
            ),
        )(tokens, queries, key_rows, cotangent, segments, levels, scales)

    three = P(("grp", "in"), None, None)
    return jax.shard_map(
        step,
        mesh=mesh,
        in_specs=(three, three, three, three, P(("grp", "in"), None), P("in", None, None), P("in", None)),
        out_specs=(three, three, three, P("grp", "in")),
        check_vma=False,
    )
```

time: 198 us -> 46.6 us (0.24)
  blocking collectives: 66.7 us -> 0 us
  other arithmetic: 53.7 us -> 0 us
  Pallas kernels: 0 us -> 36.2 us
  local copies, waits for them, and re-layouts: 33.9 us -> 9.36 us
  matrix products: 16.1 us -> 0 us
  between operations: 14.2 us -> 0.66 us
  starting transfers between devices: 11.4 us -> 0 us
    all_gather x1 -> x0, blocking collectives: 66.7 us -> none  [per_device(): scale_piece = lax.all_gather(scales, 'in', axis=0, tiled=True)]
    unnamed x2 -> x0, other arithmetic: 48.7 us -> none
    pallas_call x0 -> x1, Pallas kernels: none -> 36.2 us  [step(): pl.pallas_call(functools.partial(kernel, (Y, X, Z, heads, L, hd)), out_sh...]
    dot_general x6 -> x0, matrix products: 14.6 us -> none  [the longest x1 3.75 us: per_device(): jnp.dot(value_grad.T, tokens_one, preferred_element_type=jnp.float32)]
    unnamed x19 -> x18, local copies, waits for them, and re-layouts: 21.1 us -> 9.36 us
    all_to_all x2 -> x0, starting transfers between devices: 11.4 us -> none  [the longest x1 7.36 us: per_device(): lax.all_to_all(term[None], 'in', split_axis=2, concat_axis=0, tiled=True)]
    broadcast_in_dim x2 -> x0, local copies, waits for them, and re-layouts: 10 us -> none  [the longest x1 9.51 us: per_device(): term[None]]
    convert_element_type x4 -> x0, local copies, waits for them, and re-layouts: 2.8 us -> none  [the longest x2 1.88 us: per_device(): query_grad.reshape(length, heads * head_size).astype(jnp.bfloat16)]
  transfers between devices with their start and end apart: 3 -> 0, of which waited for: 0 -> 0; matrix products, arithmetic and copies ran while one was open for 44% -> 0% of each run, Pallas kernels for 0% -> 0%
where the time goes in v1:
time: 46.6 us; the launch traced here: 46.2 us
  Pallas kernels  36.2 us (78%)
  local copies, waits for them, and re-layouts  9.36 us (20%)
  between operations  0.66 us (1%)
    pallas_call x1, Pallas kernels, step(): pl.pallas_call(functools.partial(kernel, (Y, X, Z, heads, L, hd)), out_sh...  36.2 us
    unnamed x18, local copies, waits for them, and re-layouts  9.36 us

profile of v1, /device:TPU:0, one launch (start us, length us, event | category | flops | bytes accessed | tf_op | source)
XLA Modules:
  0.0 46.2 jit_solution(8432801902815416918)
XLA Ops:
  0.6 0.0 copy-start
  0.6 1.7 %copy-done = bf16[1,144,8192]{2,1,0:T(8,128)(2,1)S(1)} copy-done((bf16[1,144,8192]{2,1,0:T(8,128)(2,1)S(1)}, bf16[1,144,8192]{2,1,0:T(8,128)(2,1)}, u32[]{:S(2)}) %copy-start) | copy-done | bytes 2359320
  2.3 0.0 copy-start.1
  2.3 1.0 %copy-done.1 = bf16[1,144,1024]{2,1,0:T(8,128)(2,1)S(1)} copy-done((bf16[1,144,1024]{2,1,0:T(8,128)(2,1)S(1)}, bf16[1,144,1024]{2,1,0:T(8,128)(2,1)}, u32[]{:S(2)}) %copy-start.1) | copy-done | bytes 294936
  3.3 0.0 copy-start.2
  3.3 1.0 %copy-done.2 = bf16[1,144,1024]{2,1,0:T(8,128)(2,1)S(1)} copy-done((bf16[1,144,1024]{2,1,0:T(8,128)(2,1)S(1)}, bf16[1,144,1024]{2,1,0:T(8,128)(2,1)}, u32[]{:S(2)}) %copy-start.2) | copy-done | bytes 294936
  4.2 0.0 copy-start.3
  4.2 0.9 %copy-done.3 = bf16[8,128,128]{2,1,0:T(8,128)(2,1)S(1)} copy-done((bf16[8,128,128]{2,1,0:T(8,128)(2,1)S(1)}, bf16[8,128,128]{2,1,0:T(8,128)(2,1)}, u32[]{:S(2)}) %copy-start.3) | copy-done | bytes 262168
  5.2 0.0 copy-start.4
  5.2 0.8 %copy-done.4 = bf16[1,144,128]{2,1,0:T(8,128)(2,1)S(1)} copy-done((bf16[1,144,128]{2,1,0:T(8,128)(2,1)S(1)}, bf16[1,144,128]{2,1,0:T(8,128)(2,1)}, u32[]{:S(2)}) %copy-start.4) | copy-done | bytes 36888
  5.9 0.0 copy-start.5
  5.9 0.7 %copy-done.5 = bf16[8,128]{1,0:T(8,128)(2,1)S(1)} copy-done((bf16[8,128]{1,0:T(8,128)(2,1)S(1)}, bf16[8,128]{1,0:T(8,128)(2,1)}, u32[]{:S(2)}) %copy-start.5) | copy-done | bytes 2072
  6.6 0.0 copy-start.6
  6.6 0.7 %copy-done.6 = s32[1,144]{1,0:T(1,128)S(1)} copy-done((s32[1,144]{1,0:T(1,128)S(1)}, s32[1,144]{1,0:T(1,128)}, u32[]{:S(2)}) %copy-start.6) | copy-done | bytes 600
  7.3 36.2 %shard_map.102 = (bf16[1,144,1024]{2,1,0:T(8,128)(2,1)S(1)}, bf16[1,144,1024]{2,1,0:T(8,128)(2,1)S(1)}, bf16[1,144,128]{2,1,0:T(8,128)(2,1)S(1)}, f32[32,1024]{1,0:T(8,128)S(1)}) custom-call(bf16[1,144,8192]{2,1,0:T(8,128)(2,1)S(1)} %copy-done, bf16[1,144,1024]{2,1,0:T(8,128)(2,1)S(1)} %copy-done.1, bf16[1,144,128]{2,1,0:T(8,128)(2,1)S(1)} %copy-done.4, ...), custom_call_target="tpu_custom_call" | custom-call | flops 858783744 | bytes 8000000 | tf_op jit(solution)/shard_map/pallas_call | solution.py:262
  43.5 0.7 %copy.15 = bf16[1,144,1024]{2,1,0:T(8,128)(2,1)} copy(bf16[1,144,1024]{2,1,0:T(8,128)(2,1)S(1)} %get-tuple-element.8) | data formatting | bytes 589824
  44.3 0.7 %copy.16 = bf16[1,144,1024]{2,1,0:T(8,128)(2,1)} copy(bf16[1,144,1024]{2,1,0:T(8,128)(2,1)S(1)} %get-tuple-element.9) | data formatting | bytes 589824
  45.0 0.6 %copy.17 = bf16[1,144,128]{2,1,0:T(8,128)(2,1)} copy(bf16[1,144,128]{2,1,0:T(8,128)(2,1)S(1)} %get-tuple-element.10) | data formatting | bytes 73728
  45.6 0.7 %copy.18 = f32[32,1024]{1,0:T(8,128)} copy(f32[32,1024]{1,0:T(8,128)S(1)} %get-tuple-element.11) | data formatting | bytes 262144
Async XLA Ops:
  0.6 1.7 %copy-start = (bf16[1,144,8192]{2,1,0:T(8,128)(2,1)S(1)}, bf16[1,144,8192]{2,1,0:T(8,128)(2,1)}, u32[]{:S(2)}) copy-start(bf16[1,144,8192]{2,1,0:T(8,128)(2,1)} %tok_hbm.1) | copy-start | bytes 7077892
  2.3 1.0 %copy-start.1 = (bf16[1,144,1024]{2,1,0:T(8,128)(2,1)S(1)}, bf16[1,144,1024]{2,1,0:T(8,128)(2,1)}, u32[]{:S(2)}) copy-start(bf16[1,144,1024]{2,1,0:T(8,128)(2,1)} %q_hbm.1) | copy-start | bytes 884740
  3.3 1.0 %copy-start.2 = (bf16[1,144,1024]{2,1,0:T(8,128)(2,1)S(1)}, bf16[1,144,1024]{2,1,0:T(8,128)(2,1)}, u32[]{:S(2)}) copy-start(bf16[1,144,1024]{2,1,0:T(8,128)(2,1)} %cot_hbm.1) | copy-start | bytes 884740
  4.2 0.9 %copy-start.3 = (bf16[8,128,128]{2,1,0:T(8,128)(2,1)S(1)}, bf16[8,128,128]{2,1,0:T(8,128)(2,1)}, u32[]{:S(2)}) copy-start(bf16[8,128,128]{2,1,0:T(8,128)(2,1)} %lev_hbm.1) | copy-start | bytes 786436
  5.2 0.8 %copy-start.4 = (bf16[1,144,128]{2,1,0:T(8,128)(2,1)S(1)}, bf16[1,144,128]{2,1,0:T(8,128)(2,1)}, u32[]{:S(2)}) copy-start(bf16[1,144,128]{2,1,0:T(8,128)(2,1)} %k_ref.1) | copy-start | bytes 110596
  5.9 0.7 %copy-start.5 = (bf16[8,128]{1,0:T(8,128)(2,1)S(1)}, bf16[8,128]{1,0:T(8,128)(2,1)}, u32[]{:S(2)}) copy-start(bf16[8,128]{1,0:T(8,128)(2,1)} %sca_ref.1) | copy-start | bytes 6148
  6.6 0.7 %copy-start.6 = (s32[1,144]{1,0:T(1,128)S(1)}, s32[1,144]{1,0:T(1,128)}, u32[]{:S(2)}) copy-start(s32[1,144]{1,0:T(1,128)} %seg_ref.1) | copy-start | bytes 1732

commit v2 on v1

--- a/solution.py
+++ b/solution.py
@@ -25,11 +25,11 @@
 
 def kernel(
     dims,
-    tok_hbm, q_hbm, k_ref, cot_hbm, seg_ref, lev_hbm, sca_ref,
+    tok_hbm, q_hbm, k_hbm, cot_hbm, seg_hbm, lev_hbm, sca_hbm,
     att_hbm, qg_hbm, kg_hbm, wg_hbm,
-    tok, qs, cs, lev, wbuf, probs, probs_low, sg_low,
-    term_send, term_own, term_recv, sum_core, y_recv, sum_y, x_recv, sum_x, z_recv,
-    att_v, qg_v, kg_v, wg_v,
+    att_v, qg_v, kg_v, wg_v, key_v, seg_v, sca_v, tok, qs, cs, lev, wbuf, probs, probs_low, sg_low,
+    term_send, term_own, term_recv, sum_core,
+    ya_recv, xb_recv, sum_a, sum_b, xa_recv, yb_recv, sum_z, z_recv,
     in_sem, q_sem, c_sem, out_sem,
     core_s, core_r, ys_s, ys_r, xs_s, xs_r, zs_s, zs_r,
     gz_s, gz_r, gx_s, gx_r, gc_s, gc_r,
@@ -53,6 +53,12 @@
 
     lev_cp = pltpu.make_async_copy(lev_hbm, lev, in_sem.at[0])
     lev_cp.start()
+    sca_cp = pltpu.make_async_copy(sca_hbm, sca_v, in_sem.at[2])
+    sca_cp.start()
+    key_cp = pltpu.make_async_copy(k_hbm.at[0], key_v, in_sem.at[3])
+    key_cp.start()
+    seg_cp = pltpu.make_async_copy(seg_hbm, seg_v, in_sem.at[4])
+    seg_cp.start()
     q_cps, c_cps = [], []
     for h in range(heads):
         q_cps.append(pltpu.make_async_copy(
@@ -75,7 +81,8 @@
 
     lev_cp.wait()
     blocks, block_rows = lev.shape[0], lev.shape[1]
-    sca = sca_ref[...].astype(F32)
+    sca_cp.wait()
+    sca = sca_v[...].astype(F32)
     if blocks > 1:
         hb = blocks // 2
         s_half = jnp.where(c == 0, sca[:hb], sca[hb:])
@@ -89,6 +96,11 @@
     pl.semaphore_wait(barrier, len(peers))
 
     sends = []
+    outs = []
+
+    def out(src, dst, k):
+        outs.append(pltpu.make_async_copy(src, dst, out_sem.at[k]))
+        outs[-1].start()
 
     def start(cp):
         cp.start()
@@ -125,13 +137,15 @@
 
     wide = heads * L
     factor = hd ** -0.5
-    keys = k_ref[0]
+    key_cp.wait()
+    seg_cp.wait()
+    keys = key_v[...]
     lane = lax.broadcasted_iota(jnp.int32, (1, wide), 1)
     s_pos = lane
     for h in range(1, heads):
         s_pos = jnp.where(lane >= h * L, lane - h * L, s_pos)
     t_pos = lax.broadcasted_iota(jnp.int32, (L, 1), 0)
-    seg_row = seg_ref[...].astype(F32)
+    seg_row = seg_v[...].astype(F32)
     sq_r = lax.broadcasted_iota(jnp.int32, (L, L), 0)
     sq_c = lax.broadcasted_iota(jnp.int32, (L, L), 1)
     seg_col = jnp.sum(jnp.where(sq_r == sq_c, seg_row, 0.0), axis=1, keepdims=True)
@@ -154,43 +168,81 @@
 
     tok_cp.wait()
     half = Y * r
-    for zz in range(Z):
+    z_half = (Z + 1) // 2
+    order = [zz for k in range(z_half) for zz in (k, k + z_half) if zz < Z]
+
+    def y_copy(zz, d):
+        if zz < z_half:
+            src, dst = sum_core.at[zz, lax.rem(y + d, Y)], ya_recv.at[zz, d]
+        else:
+            src, dst = sum_b.at[zz, lax.rem(y + d, Y)], yb_recv.at[zz, d]
+        return remote(src, dst, ys_s.at[zz, d], ys_r.at[zz, d], y_dev(d))
+
+    def x_copy(zz, d):
+        if zz < z_half:
+            src, dst = sum_a.at[zz, lax.rem(x + d, X)], xa_recv.at[zz, d]
+        else:
+            src, dst = sum_core.at[zz, :, lax.rem(x + d, X)], xb_recv.at[zz, d]
+        return remote(src, dst, xs_s.at[zz, d], xs_r.at[zz, d], x_dev(d))
+
+    def core_copy(zz):
+        return remote(term_send.at[zz], term_recv.at[zz], core_s.at[zz], core_r.at[zz], core_dev)
+
+    for zz in order:
         for xx in range(X):
             at = (zz * X + xx) * c_w
             t = dot(vg_rows, tok[:, at:at + c_w], 1, 0)
             term_send[zz, :, xx] = t[:half].reshape(Y, r, c_w).astype(BF16)
             term_own[zz, :, xx] = t[half:].reshape(Y, r, c_w)
-        start(remote(term_send.at[zz], term_recv.at[zz], core_s.at[zz], core_r.at[zz], core_dev))
-
-    for zz in range(Z):
-        remote(term_send.at[zz], term_recv.at[zz], core_s.at[zz], core_r.at[zz], core_dev).wait_recv()
+        start(core_copy(zz))
+
+    for zz in order:
+        core_copy(zz).wait_recv()
         sum_core[zz] = (term_own[zz] + term_recv[zz].astype(F32)).astype(BF16)
-        for d in range(1, Y):
-            start(remote(sum_core.at[zz, lax.rem(y + d, Y)], y_recv.at[zz, d],
-                         ys_s.at[zz, d], ys_r.at[zz, d], y_dev(d)))
-
-    for zz in range(Z):
-        total = sum_core[zz, y].astype(F32)
-        for d in range(1, Y):
-            remote(y_recv.at[zz, d], y_recv.at[zz, d], ys_s.at[zz, d], ys_r.at[zz, d], y_dev(d)).wait_recv()
-            total = total + y_recv[zz, d].astype(F32)
-        sum_y[zz] = total.astype(BF16)
-        for d in range(1, X):
-            start(remote(sum_y.at[zz, lax.rem(x + d, X)], x_recv.at[zz, d],
-                         xs_s.at[zz, d], xs_r.at[zz, d], x_dev(d)))
-        if zz + 1 < Z:
-            wait_z(zz + 1)
-            forward_x(zz + 1)
-            forward_core(zz + 1, 0)
-
-    for zz in range(Z):
-        total = sum_y[zz, x].astype(F32)
-        for d in range(1, X):
-            remote(x_recv.at[zz, d], x_recv.at[zz, d], xs_s.at[zz, d], xs_r.at[zz, d], x_dev(d)).wait_recv()
-            total = total + x_recv[zz, d].astype(F32)
-        sum_x[zz] = total.astype(BF16)
-    for d in range(1, Z):
-        start(remote(sum_x.at[lax.rem(z + d, Z)], z_recv.at[d], zs_s.at[d], zs_r.at[d], z_dev(d)))
+        for d in range(1, Y if zz < z_half else X):
+            start(y_copy(zz, d) if zz < z_half else x_copy(zz, d))
+
+    gathered = 0
+    for zz in order:
+        if zz < z_half:
+            total = sum_core[zz, y].astype(F32)
+            for d in range(1, Y):
+                y_copy(zz, d).wait_recv()
+                total = total + ya_recv[zz, d].astype(F32)
+            sum_a[zz] = total.astype(BF16)
+            for d in range(1, X):
+                start(x_copy(zz, d))
+        else:
+            total = sum_core[zz, :, x].astype(F32)
+            for d in range(1, X):
+                x_copy(zz, d).wait_recv()
+                total = total + xb_recv[zz, d].astype(F32)
+            sum_b[zz] = total.astype(BF16)
+            for d in range(1, Y):
+                start(y_copy(zz, d))
+        gathered += 1
+        if gathered < Z:
+            wait_z(gathered)
+            forward_x(gathered)
+            forward_core(gathered, 0)
+
+    for zz in order:
+        if zz < z_half:
+            total = sum_a[zz, x].astype(F32)
+            for d in range(1, X):
+                x_copy(zz, d).wait_recv()
+                total = total + xa_recv[zz, d].astype(F32)
+        else:
+            total = sum_b[zz, y].astype(F32)
+            for d in range(1, Y):
+                y_copy(zz, d).wait_recv()
+                total = total + yb_recv[zz, d].astype(F32)
+        sum_z[zz] = total.astype(BF16)
+
+        @pl.when(z != zz)
+        def _():
+            d = lax.rem(zz + Z - z, Z)
+            remote(sum_z.at[zz], z_recv.at[d], zs_s.at[d], zs_r.at[d], z_dev(d)).start()
 
     values = jnp.zeros((L, hd), F32)
     piece_rows = 2 * wbuf.shape[2]
@@ -211,12 +263,10 @@
         values = values + dot(tok[:, cols], wbuf[p].reshape(piece_rows, hd), 1, 0)
     v_low = values.astype(BF16)
 
-    outs = []
     att = dot(probs_low[...], v_low, 0, 0).astype(BF16)
     for h in range(heads):
         att_v[:, h * hd:(h + 1) * hd] = att[h * L:(h + 1) * L]
-    outs.append(pltpu.make_async_copy(att_v, att_hbm.at[0], out_sem.at[0]))
-    outs[-1].start()
+    out(att_v, att_hbm.at[0], 0)
     pg = dot(v_low, cs[...], 1, 1)
     weighted = probs[...] * pg
     centre = jnp.sum(weighted, axis=0, keepdims=True)
@@ -224,22 +274,34 @@
     qg = dot(sg_low[...], keys, 0, 0).astype(BF16)
     for h in range(heads):
         qg_v[:, h * hd:(h + 1) * hd] = qg[h * L:(h + 1) * L]
-    outs.append(pltpu.make_async_copy(qg_v, qg_hbm.at[0], out_sem.at[1]))
-    outs[-1].start()
+    out(qg_v, qg_hbm.at[0], 1)
     kg_v[...] = dot(sg_low[...], qs[...], 1, 0).astype(BF16)
-    outs.append(pltpu.make_async_copy(kg_v, kg_hbm.at[0], out_sem.at[2]))
-    outs[-1].start()
-
-    total = sum_x[z].astype(F32)
+    out(kg_v, kg_hbm.at[0], 2)
+
+    total = sum_z[z].astype(F32)
     for d in range(1, Z):
         remote(z_recv.at[d], z_recv.at[d], zs_s.at[d], zs_r.at[d], z_dev(d)).wait_recv()
         total = total + z_recv[d].astype(F32)
     wg_v[...] = total * (1.0 / (2 * Y * X * Z))
-    outs.append(pltpu.make_async_copy(wg_v, wg_hbm, out_sem.at[3]))
-    outs[-1].start()
+    out(wg_v, wg_hbm, 3)
     for cp in sends:
         cp.wait_send()
+    for d in range(1, Z):
+        remote(sum_z.at[0], z_recv.at[d], zs_s.at[d], zs_r.at[d], z_dev(d)).wait_send()
     for cp in outs:
+        cp.wait()
+
+
+def write_out(*refs):
+    held, sems = refs[8:12], refs[12]
+    into = [pltpu.make_async_copy(refs[k], held[k], sems.at[k]) for k in range(4)]
+    away = [pltpu.make_async_copy(held[k], refs[4 + k], sems.at[4 + k]) for k in range(4)]
+    for cp in into:
+        cp.start()
+    for a, b in zip(into, away):
+        a.wait()
+        b.start()
+    for cp in away:
         cp.wait()
 
 
@@ -256,10 +318,9 @@
         wide = heads * L
         r, c_w = hd // n_grp, D // n_in
         half_rows = c_w // 2
-        any_spec = pl.BlockSpec(memory_space=pl.ANY)
-        vmem = pl.BlockSpec(memory_space=pltpu.VMEM)
+        hbm = pl.BlockSpec(memory_space=pltpu.HBM)
         DMA = pltpu.SemaphoreType.DMA
-        return pl.pallas_call(
+        results = pl.pallas_call(
             functools.partial(kernel, (Y, X, Z, heads, L, hd)),
             out_shape=(
                 jax.ShapeDtypeStruct(queries.shape, BF16),
@@ -267,9 +328,16 @@
                 jax.ShapeDtypeStruct(key_rows.shape, BF16),
                 jax.ShapeDtypeStruct((r, c_w), F32),
             ),
-            in_specs=[any_spec, any_spec, vmem, any_spec, vmem, any_spec, vmem],
-            out_specs=(any_spec,) * 4,
+            in_specs=[hbm] * 7,
+            out_specs=(hbm,) * 4,
             scratch_shapes=[
+                pltpu.VMEM((L, heads * hd), BF16),
+                pltpu.VMEM((L, heads * hd), BF16),
+                pltpu.VMEM((L, hd), BF16),
+                pltpu.VMEM((r, c_w), F32),
+                pltpu.VMEM((L, hd), BF16),
+                pltpu.VMEM((1, L), jnp.int32),
+                pltpu.VMEM(scales.shape, BF16),
                 pltpu.VMEM((L, D), BF16),
                 pltpu.VMEM((wide, hd), BF16),
                 pltpu.VMEM((wide, hd), BF16),
@@ -283,15 +351,14 @@
                 pltpu.VMEM((Z, Y, X, r, c_w), BF16),
                 pltpu.VMEM((Z, Y, X, r, c_w), BF16),
                 pltpu.VMEM((Z, Y, X, r, c_w), BF16),
+                pltpu.VMEM((Z, X, Y, r, c_w), BF16),
                 pltpu.VMEM((Z, X, r, c_w), BF16),
+                pltpu.VMEM((Z, Y, r, c_w), BF16),
                 pltpu.VMEM((Z, X, r, c_w), BF16),
+                pltpu.VMEM((Z, Y, r, c_w), BF16),
                 pltpu.VMEM((Z, r, c_w), BF16),
                 pltpu.VMEM((Z, r, c_w), BF16),
-                pltpu.VMEM((L, heads * hd), BF16),
-                pltpu.VMEM((L, heads * hd), BF16),
-                pltpu.VMEM((L, hd), BF16),
-                pltpu.VMEM((r, c_w), F32),
-                DMA((2,)), DMA((heads,)), DMA((heads,)), DMA((4,)),
+                DMA((5,)), DMA((heads,)), DMA((heads,)), DMA((4,)),
                 DMA((Z,)), DMA((Z,)),
                 DMA((Z, Y)), DMA((Z, Y)),
                 DMA((Z, X)), DMA((Z, X)),
@@ -301,13 +368,21 @@
                 DMA((Z, X)), DMA((Z, X)),
             ],
             compiler_params=pltpu.CompilerParams(
-                collective_id=0, has_side_effects=True, vmem_limit_bytes=40 * 1024 * 1024
+                collective_id=0, has_side_effects=True, vmem_limit_bytes=56 * 1024 * 1024
             ),
             cost_estimate=pl.CostEstimate(
                 flops=2 * L * D * hd * 2 + 12 * heads * L * L * hd,
                 bytes_accessed=8_000_000, transcendentals=heads * L * L,
             ),
         )(tokens, queries, key_rows, cotangent, segments, levels, scales)
+        return pl.pallas_call(
+            write_out,
+            out_shape=tuple(jax.ShapeDtypeStruct(a.shape, a.dtype) for a in results),
+            in_specs=[hbm] * 4,
+            out_specs=(hbm,) * 4,
+            scratch_shapes=[pltpu.VMEM(a.shape, a.dtype) for a in results] + [DMA((8,))],
+            compiler_params=pltpu.CompilerParams(vmem_limit_bytes=56 * 1024 * 1024),
+        )(*results)
 
     three = P(("grp", "in"), None, None)
     return jax.shard_map(

time: 46.6 us -> 33.6 us (0.72)
  local copies, waits for them, and re-layouts: 9.36 us -> 0 us
  Pallas kernels: 36.2 us -> 32.7 us
    unnamed x18 -> x0, local copies, waits for them, and re-layouts: 9.36 us -> none
    pallas_call x1, Pallas kernels: 36.2 us -> 30.8 us  [step(): pl.pallas_call(functools.partial(kernel, (Y, X, Z, heads, L, hd)), out_sh...]
    pallas_call x0 -> x1, Pallas kernels: none -> 1.89 us  [step(): pl.pallas_call(write_out, out_shape=tuple((jax.ShapeDtypeStruct(a.shape,...]
where the time goes in v2:
time: 33.6 us; the launch traced here: 33.3 us
  Pallas kernels  32.7 us (97%)
  between operations  0.64 us (2%)
    pallas_call x1, Pallas kernels, step(): pl.pallas_call(functools.partial(kernel, (Y, X, Z, heads, L, hd)), out_sh...  30.8 us
    pallas_call x1, Pallas kernels, step(): pl.pallas_call(write_out, out_shape=tuple((jax.ShapeDtypeStruct(a.shape,...  1.89 us

profile of v2, /device:TPU:0, one launch (start us, length us, event | category | flops | bytes accessed | tf_op | source)
XLA Modules:
  0.0 33.3 jit_solution(8685321693547239707)
XLA Ops:
  0.6 30.8 %shard_map.102 = (bf16[1,144,1024]{2,1,0:T(8,128)(2,1)}, bf16[1,144,1024]{2,1,0:T(8,128)(2,1)}, bf16[1,144,128]{2,1,0:T(8,128)(2,1)}, f32[32,1024]{1,0:T(8,128)}) custom-call(bf16[1,144,8192]{2,1,0:T(8,128)(2,1)} %tok_hbm.1, bf16[1,144,1024]{2,1,0:T(8,128)(2,1)} %q_hbm.1, bf16[1,144,128]{2,1,0:T(8,128)(2,1)} %k_hbm.1, bf16[1,144,1024]{2,1,0:T(8,128)(2,1)} %cot_hbm.1, ...), custom_call_target="tpu_custom_call" | custom-call | flops 858783744 | bytes 8000000 | tf_op jit(solution)/shard_map/pallas_call | solution.py:323
  31.4 1.9 %shard_map.103 = (bf16[1,144,1024]{2,1,0:T(8,128)(2,1)}, bf16[1,144,1024]{2,1,0:T(8,128)(2,1)}, bf16[1,144,128]{2,1,0:T(8,128)(2,1)}, f32[32,1024]{1,0:T(8,128)}) custom-call(bf16[1,144,1024]{2,1,0:T(8,128)(2,1)} %get-tuple-element.8.refs_0_, bf16[1,144,1024]{2,1,0:T(8,128)(2,1)} %get-tuple-element.9.refs_1_, ...), custom_call_target="tpu_custom_call" | custom-call | tf_op jit(solution)/shard_map/pallas_call | solution.py:378

commit v3 on v2

--- a/solution.py
+++ b/solution.py
@@ -188,6 +188,13 @@
     def core_copy(zz):
         return remote(term_send.at[zz], term_recv.at[zz], core_s.at[zz], core_r.at[zz], core_dev)
 
+    def join_cores(zz):
+        core_copy(zz).wait_recv()
+        sum_core[zz] = (term_own[zz] + term_recv[zz].astype(F32)).astype(BF16)
+        for d in range(1, Y if zz < z_half else X):
+            start(y_copy(zz, d) if zz < z_half else x_copy(zz, d))
+
+    before = None
     for zz in order:
         for xx in range(X):
             at = (zz * X + xx) * c_w
@@ -195,12 +202,10 @@
             term_send[zz, :, xx] = t[:half].reshape(Y, r, c_w).astype(BF16)
             term_own[zz, :, xx] = t[half:].reshape(Y, r, c_w)
         start(core_copy(zz))
-
-    for zz in order:
-        core_copy(zz).wait_recv()
-        sum_core[zz] = (term_own[zz] + term_recv[zz].astype(F32)).astype(BF16)
-        for d in range(1, Y if zz < z_half else X):
-            start(y_copy(zz, d) if zz < z_half else x_copy(zz, d))
+        if before is not None:
+            join_cores(before)
+        before = zz
+    join_cores(before)
 
     gathered = 0
     for zz in order:

time: 33.6 us -> 33.5 us (level)
  no operation moved by 1% of the time
where the time goes in v3:
time: 33.5 us; the launch traced here: 33.3 us
  Pallas kernels  32.7 us (98%)
  between operations  0.64 us (2%)
    pallas_call x1, Pallas kernels, step(): pl.pallas_call(functools.partial(kernel, (Y, X, Z, heads, L, hd)), out_sh...  30.8 us
    pallas_call x1, Pallas kernels, step(): pl.pallas_call(write_out, out_shape=tuple((jax.ShapeDtypeStruct(a.shape,...  1.89 us

profile of v3, /device:TPU:0, one launch (start us, length us, event | category | flops | bytes accessed | tf_op | source)
XLA Modules:
  0.0 33.3 jit_solution(1902441411655043097)
XLA Ops:
  0.6 30.8 %shard_map.102 = (bf16[1,144,1024]{2,1,0:T(8,128)(2,1)}, bf16[1,144,1024]{2,1,0:T(8,128)(2,1)}, bf16[1,144,128]{2,1,0:T(8,128)(2,1)}, f32[32,1024]{1,0:T(8,128)}) custom-call(bf16[1,144,8192]{2,1,0:T(8,128)(2,1)} %tok_hbm.1, bf16[1,144,1024]{2,1,0:T(8,128)(2,1)} %q_hbm.1, bf16[1,144,128]{2,1,0:T(8,128)(2,1)} %k_hbm.1, bf16[1,144,1024]{2,1,0:T(8,128)(2,1)} %cot_hbm.1, ...), custom_call_target="tpu_custom_call" | custom-call | flops 858783744 | bytes 8000000 | tf_op jit(solution)/shard_map/pallas_call | solution.py:328
  31.4 1.9 %shard_map.103 = (bf16[1,144,1024]{2,1,0:T(8,128)(2,1)}, bf16[1,144,1024]{2,1,0:T(8,128)(2,1)}, bf16[1,144,128]{2,1,0:T(8,128)(2,1)}, f32[32,1024]{1,0:T(8,128)}) custom-call(bf16[1,144,1024]{2,1,0:T(8,128)(2,1)} %get-tuple-element.8.refs_0_, bf16[1,144,1024]{2,1,0:T(8,128)(2,1)} %get-tuple-element.9.refs_1_, ...), custom_call_target="tpu_custom_call" | custom-call | tf_op jit(solution)/shard_map/pallas_call | solution.py:383
